TPU v7x, 32 devices: a whole 2x2x4 slice. The times are simulated.
32 devices in a mesh: scene: 2 (over x), gx: 16 (over z, y, core).
Axes of the slice: x: 2, y: 2, z: 4, core: 2. Of those that a mesh axis runs over, the one named last changes fastest.
Arguments:
- cotangent: float32 [128, 128, 256], P(('scene', 'gx')), parts along dimension 0, may hold values from -24 to 24
- counts: int32 [128, 128, 256], P(('scene', 'gx')), parts along dimension 0, may hold values from 0 to 31
Outputs:
- multiplier: float32 [128, 128, 256], P(('scene', 'gx')), parts along dimension 0
- normal_grad: float32 [3, 128, 128, 256], P(None, ('scene', 'gx')), parts along dimension 1
There are 2 independent parts, one for each index of `scene`. A program takes and returns all parts, laid end to end along the dimension named above; each array names one. Nothing has to cross between parts.
All inputs are finite; a program needn't handle non-finite values.
Results may differ from a plain program's by a relative error of at most 0.0001.
Values sent between devices are 32-bit elements; how exact they have to be, the bound alone decides.
A program may use at most 128 MiB of HBM per device.

v0:
```python
import jax
import jax.numpy as jnp
from jax import lax
from jax.sharding import PartitionSpec as P

SWEEPS = 2
COARSE = 16
CYCLES = 2


damping = 0.8
screen_rate = 0.004


def extended(array, sides, width):
    for axis, dim in sides:
        size, length = (lax.axis_size(axis), array.shape[dim])
        up = [(i, (i + 1) % size) for i in range(size - 1)]
        down = [(j, i) for i, j in up]
        last = lax.slice_in_dim(array, length - width, length, axis=dim)
        initial = lax.slice_in_dim(array, 0, width, axis=dim)
        before = lax.ppermute(last, axis, up)
        after = lax.ppermute(initial, axis, down)
        array = jnp.concatenate([before, array, after], axis=dim)
    return array


def passed_along(array, axis, by):
    length = lax.axis_size(axis)
    pairs = [(i, i + by) for i in range(length) if 0 <= i + by < length]
    return lax.ppermute(array, axis, pairs)


def stencil(padded, field, weight, inv_h2):
    padded = jnp.pad(padded, ((0, 0), (1, 1), (1, 1)))
    beside = padded[2:, 1:-1, 1:-1] + padded[:-2, 1:-1, 1:-1]
    beside = beside + padded[1:-1, 2:, 1:-1] + padded[1:-1, :-2, 1:-1]
    beside = beside + padded[1:-1, 1:-1, 2:] + padded[1:-1, 1:-1, :-2]
    return inv_h2 * (6.0 * field - beside) + weight * field


def apply_fine(field, weight):
    padded = extended(field, (("gx", 0),), 1)
    return stencil(padded, field, weight, 1.0)


def apply_middle(field, weight):
    padded = extended(field, (("gx", 0),), 1)
    return stencil(padded, field, weight, 0.25)


def restrict(field):
    sx, sy, sz = field.shape
    return field.reshape(sx // 2, 2, sy // 2, 2, sz // 2, 2).mean(axis=(1, 3, 5))


def prolong(field):
    return jnp.repeat(jnp.repeat(jnp.repeat(field, 2, axis=0), 2, axis=1), 2, axis=2)


def shards(cotangent, counts):
    screen_fine = screen_rate * counts.astype(jnp.float32)
    screen_mid = restrict(screen_fine)
    screen_low = restrict(screen_mid)
    low_h2 = 0.0625

    def coarse_solve(source):

        def slab_sweep(_, field):
            padded = extended(field, (("gx", 0),), 1)
            update = source - stencil(padded, field, screen_low, low_h2)
            return field + damping * update / (6.0 * low_h2 + screen_low)

        return lax.fori_loop(0, COARSE, slab_sweep, jnp.zeros_like(source))

    def smooth_fine(field, source):
        return field + damping * (source - apply_fine(field, screen_fine)) / (6.0 + screen_fine)

    def smooth_middle(field, source):
        return field + damping * (source - apply_middle(field, screen_mid)) / (
            6.0 * 0.25 + screen_mid
        )

    def vcycle(field, source):
        for _ in range(SWEEPS):
            field = smooth_fine(field, source)
        mid_rhs = restrict(source - apply_fine(field, screen_fine))
        error = jnp.zeros_like(mid_rhs)
        for _ in range(SWEEPS):
            error = smooth_middle(error, mid_rhs)
        low_rhs = restrict(mid_rhs - apply_middle(error, screen_mid))
        error = error + prolong(coarse_solve(low_rhs))
        for _ in range(SWEEPS):
            error = smooth_middle(error, mid_rhs)
        field = field + prolong(error)
        for _ in range(SWEEPS):
            field = smooth_fine(field, source)
        return field

    multiplier = jnp.zeros_like(cotangent)
    for _ in range(CYCLES):
        multiplier = vcycle(multiplier, cotangent)
    following = passed_along(multiplier[:1], "gx", -1)
    ahead_x = jnp.concatenate([multiplier[1:], following], axis=0)
    ahead_y = jnp.pad(multiplier[:, 1:], ((0, 0), (0, 1), (0, 0)))
    ahead_z = jnp.pad(multiplier[:, :, 1:], ((0, 0), (0, 0), (0, 1)))
    normal_grad = jnp.stack([multiplier - ahead_x, multiplier - ahead_y, multiplier - ahead_z])
    return (multiplier, normal_grad)


def solution(mesh):
    placed = (P(("scene", "gx"), None, None), P(("scene", "gx"), None, None))
    return jax.shard_map(
        shards,
        mesh=mesh,
        in_specs=placed,
        out_specs=(P(("scene", "gx"), None, None), P(None, ("scene", "gx"), None, None)),
        check_vma=False,
    )
```

profile of v0, /device:TPU:1, one launch (start us, length us, event | category | flops | bytes accessed | tf_op | source)
XLA Modules:
  0.0 595.1 jit_solution(14016264479452969478)
XLA Ops:
  30.0 34.9 %reshape.100 = f32[2,2,64,2,128,2]{5,4,3,2,1,0:T(8,128)} reshape(f32[4,128,256]{2,1,0:T(8,128)S(1)} %copy.27) | data formatting | bytes 1048576 | tf_op jit(solution)/shard_map/reshape | solution.py:54
  64.9 12.2 %reduce_sum.61 = f32[2,64,128]{2,1,0:T(8,128)S(1)} reduce(f32[2,2,64,2,128,2]{5,4,3,2,1,0:T(8,128)} %reshape.100, f32[]{:T(128)} %constant.95.clone.1), dimensions={1,3,5}, to_apply=%region_1.0 | reduce | flops 114688 | bytes 589828 | tf_op jit(solution)/shard_map/reduce_sum | solution.py:54
  78.5 34.9 %reshape.99 = f32[2,2,64,2,128,2]{5,4,3,2,1,0:T(8,128)} reshape(f32[4,128,256]{2,1,0:T(8,128)S(1)} %copy.26) | data formatting | bytes 1048576 | tf_op jit(solution)/shard_map/reshape | solution.py:54
  113.4 12.2 %reduce_sum.60 = f32[2,64,128]{2,1,0:T(8,128)S(1)} reduce(f32[2,2,64,2,128,2]{5,4,3,2,1,0:T(8,128)} %reshape.99, f32[]{:T(128)} %constant.95.clone.1), dimensions={1,3,5}, to_apply=%region_0.0 | reduce | flops 114688 | bytes 589828 | tf_op jit(solution)/shard_map/reduce_sum | solution.py:54
  151.5 129.3 %while.32 = (s32[]{:T(128)}, f32[1,32,64]{2,1,0:T(8,128)S(1)}, f32[1,32,64]{2,1,0:T(8,128)S(1)}, f32[1,32,64]{2,1,0:T(8,128)S(1)}, s32[]{:T(128)}, /*index=5*/s32[]{:T(128)}) while((s32[]{:T(128)}, f32[1,32,64]{2,1,0:T(8,128)S(1)}, f32[1,32,64]{2,1,0:T(8,128)S(1)}, f32[1,32,64]{2,1,0:T(8,128)S(1)}, s32[]{:T(128)}, ...), condition=%wide.region_7.8_spmd.clone, body=%wide.region_6.7_spmd.clone.sunk | while | flops 135799 | bytes 215504 | solution.py:74
  161.0 5.3 collective-permute-start.1
  169.2 5.1 collective-permute-start.1
  177.4 5.1 collective-permute-start.1
  185.5 5.1 collective-permute-start.1
  193.6 5.1 collective-permute-start.1
  201.7 5.1 collective-permute-start.1
  209.8 5.1 collective-permute-start.1
  217.9 5.1 collective-permute-start.1
  234.1 5.1 collective-permute-start.1
  242.2 5.1 collective-permute-start.1
  250.3 5.1 collective-permute-start.1
  258.4 5.1 collective-permute-start.1
  266.5 5.1 collective-permute-start.1
  274.6 5.1 collective-permute-start.1
  283.0 5.1 collective-permute-start.17
  300.0 5.1 collective-permute-start.21
  329.6 5.3 collective-permute-start.27
  339.9 5.5 collective-permute-start.29
  348.4 34.9 %reshape.104 = f32[2,2,64,2,128,2]{5,4,3,2,1,0:T(8,128)} reshape(f32[4,128,256]{2,1,0:T(8,128)S(1)} %copy.36) | data formatting | bytes 1048576 | tf_op jit(solution)/shard_map/reshape | solution.py:54
  383.3 12.2 %reduce_sum.83 = f32[2,64,128]{2,1,0:T(8,128)S(1)} reduce(f32[2,2,64,2,128,2]{5,4,3,2,1,0:T(8,128)} %reshape.104, f32[]{:T(128)} %constant.95.clone.1), dimensions={1,3,5}, to_apply=%region_8.9 | reduce | flops 114688 | bytes 589828 | tf_op jit(solution)/shard_map/reduce_sum | solution.py:54
  397.5 5.3 collective-permute-start.31
  406.0 6.0 %collective-permute-start.33 = (f32[1,64,128]{2,1,0:T(8,128)S(1)}, f32[1,64,128]{2,1,0:T(8,128)S(1)}, u32[]{:S(2)}, u32[]{:S(2)}) collective-permute-start(f32[1,64,128]{2,1,0:T(8,128)S(1)} %get-tuple-element.191), channel_id=1, source_target_pairs={{0,1},{1,2},{2,3},{3,4},{4,5},{5,6},{6,7},{7,8},{8,9},{9,10},{10,1... | collective-permute-start | bytes 98312 | tf_op jit(solution)/shard_map/ppermute | solution.py:22
  418.7 130.0 %while.33 = (s32[]{:T(128)}, f32[1,32,64]{2,1,0:T(8,128)S(1)}, f32[1,32,64]{2,1,0:T(8,128)S(1)}, f32[1,32,64]{2,1,0:T(8,128)S(1)}, s32[]{:T(128)}, /*index=5*/s32[]{:T(128)}) while((s32[]{:T(128)}, f32[1,32,64]{2,1,0:T(8,128)S(1)}, f32[1,32,64]{2,1,0:T(8,128)S(1)}, f32[1,32,64]{2,1,0:T(8,128)S(1)}, s32[]{:T(128)}, ...), condition=%wide.region_12.13_spmd.clone, body=%wide.region_11.12_spmd.clone.sunk | while | flops 135799 | bytes 215504 | solution.py:74
  420.7 5.3 collective-permute-start.3
  428.9 5.3 collective-permute-start.3
  437.2 5.1 collective-permute-start.3
  445.3 5.1 collective-permute-start.3
  (385 shorter events, 325.5 us)
Async XLA Ops:
  0.6 9.0 %collective-permute-start.4 = (f32[1,128,256]{1,2,0:T(8,128)S(1)}, f32[1,128,256]{1,2,0:T(8,128)S(1)}, u32[]{:S(2)}, u32[]{:S(2)}) collective-permute-start(f32[1,128,256]{1,2,0:T(8,128)S(1)} %broadcast.212), channel_id=1, source_target_pairs={{1,0},{2,1},{3,2},{4,3},{5,4},{6,5},{7,6},{8,7},{9,8},{10,9},{11,1... | collective-permute-start | bytes 393224 | tf_op jit(solution)/shard_map/ppermute | solution.py:23
  10.8 11.7 %collective-permute-start.6 = (f32[1,128,256]{1,2,0:T(8,128)S(1)}, f32[1,128,256]{1,2,0:T(8,128)S(1)}, u32[]{:S(2)}, u32[]{:S(2)}) collective-permute-start(f32[1,128,256]{1,2,0:T(8,128)S(1)} %get-tuple-element.186), channel_id=1, source_target_pairs={{1,0},{2,1},{3,2},{4,3},{5,4},{6,5},{7,6},{8,7},{9,8},{10,9},{11,1... | collective-permute-start | bytes 393224 | tf_op jit(solution)/shard_map/ppermute | solution.py:23
  12.7 9.8 %collective-permute-start.7 = (f32[1,128,256]{1,2,0:T(8,128)S(1)}, f32[1,128,256]{1,2,0:T(8,128)S(1)}, u32[]{:S(2)}, u32[]{:S(2)}) collective-permute-start(f32[1,128,256]{1,2,0:T(8,128)S(1)} %get-tuple-element.185), channel_id=1, source_target_pairs={{0,1},{1,2},{2,3},{3,4},{4,5},{5,6},{6,7},{7,8},{8,9},{9,10},{10,1... | collective-permute-start | bytes 393224 | tf_op jit(solution)/shard_map/ppermute | solution.py:22
  16.9 12.3 %collective-permute-start.10 = (f32[1,64,128]{2,1,0:T(8,128)S(1)}, f32[1,64,128]{2,1,0:T(8,128)S(1)}, u32[]{:S(2)}, u32[]{:S(2)}) collective-permute-start(f32[1,64,128]{2,1,0:T(8,128)S(1)} %broadcast.217), channel_id=1, source_target_pairs={{1,0},{2,1},{3,2},{4,3},{5,4},{6,5},{7,6},{8,7},{9,8},{10,9},{11,1... | collective-permute-start | bytes 98312 | tf_op jit(solution)/shard_map/ppermute | solution.py:23
  18.8 10.4 %collective-permute-start.11 = (f32[1,64,128]{2,1,0:T(8,128)S(1)}, f32[1,64,128]{2,1,0:T(8,128)S(1)}, u32[]{:S(2)}, u32[]{:S(2)}) collective-permute-start(f32[1,64,128]{2,1,0:T(8,128)S(1)} %broadcast.217), channel_id=1, source_target_pairs={{0,1},{1,2},{2,3},{3,4},{4,5},{5,6},{6,7},{7,8},{8,9},{9,10},{10,1... | collective-permute-start | bytes 98312 | tf_op jit(solution)/shard_map/ppermute | solution.py:22
  23.6 53.5 %collective-permute-start.8 = (f32[1,128,256]{1,2,0:T(8,128)S(1)}, f32[1,128,256]{1,2,0:T(8,128)S(1)}, u32[]{:S(2)}, u32[]{:S(2)}) collective-permute-start(f32[1,128,256]{1,2,0:T(8,128)S(1)} %get-tuple-element.184), channel_id=1, source_target_pairs={{1,0},{2,1},{3,2},{4,3},{5,4},{6,5},{7,6},{8,7},{9,8},{10,9},{11,1... | collective-permute-start | bytes 393224 | tf_op jit(solution)/shard_map/ppermute | solution.py:23
  25.5 51.6 %collective-permute-start.9 = (f32[1,128,256]{1,2,0:T(8,128)S(1)}, f32[1,128,256]{1,2,0:T(8,128)S(1)}, u32[]{:S(2)}, u32[]{:S(2)}) collective-permute-start(f32[1,128,256]{1,2,0:T(8,128)S(1)} %get-tuple-element.183), channel_id=1, source_target_pairs={{0,1},{1,2},{2,3},{3,4},{4,5},{5,6},{6,7},{7,8},{8,9},{9,10},{10,1... | collective-permute-start | bytes 393224 | tf_op jit(solution)/shard_map/ppermute | solution.py:22
  159.0 7.2 %collective-permute-start = (f32[1,32,64]{2,1,0:T(8,128)S(1)}, f32[1,32,64]{2,1,0:T(8,128)S(1)}, u32[]{:S(2)}, u32[]{:S(2)}) collective-permute-start(f32[1,32,64]{2,1,0:T(8,128)S(1)} %broadcast_select_fusion.4), channel_id=1, source_target_pairs={{1,0},{2,1},{3,2},{4,3},{5,4},{6,5},{7,6},{8,7},{9,8},{10,9},{11,1... | collective-permute-start | bytes 24584 | tf_op jit(solution)/shard_map/while/body/eval_jaxpr/ppermute | solution.py:23
  167.3 7.1 %collective-permute-start = (f32[1,32,64]{2,1,0:T(8,128)S(1)}, f32[1,32,64]{2,1,0:T(8,128)S(1)}, u32[]{:S(2)}, u32[]{:S(2)}) collective-permute-start(f32[1,32,64]{2,1,0:T(8,128)S(1)} %broadcast_select_fusion.4), channel_id=1, source_target_pairs={{1,0},{2,1},{3,2},{4,3},{5,4},{6,5},{7,6},{8,7},{9,8},{10,9},{11,1... | collective-permute-start | bytes 24584 | tf_op jit(solution)/shard_map/while/body/eval_jaxpr/ppermute | solution.py:23
  191.6 7.0 %collective-permute-start = (f32[1,32,64]{2,1,0:T(8,128)S(1)}, f32[1,32,64]{2,1,0:T(8,128)S(1)}, u32[]{:S(2)}, u32[]{:S(2)}) collective-permute-start(f32[1,32,64]{2,1,0:T(8,128)S(1)} %broadcast_select_fusion.4), channel_id=1, source_target_pairs={{1,0},{2,1},{3,2},{4,3},{5,4},{6,5},{7,6},{8,7},{9,8},{10,9},{11,1... | collective-permute-start | bytes 24584 | tf_op jit(solution)/shard_map/while/body/eval_jaxpr/ppermute | solution.py:23
  224.1 7.0 %collective-permute-start = (f32[1,32,64]{2,1,0:T(8,128)S(1)}, f32[1,32,64]{2,1,0:T(8,128)S(1)}, u32[]{:S(2)}, u32[]{:S(2)}) collective-permute-start(f32[1,32,64]{2,1,0:T(8,128)S(1)} %broadcast_select_fusion.4), channel_id=1, source_target_pairs={{1,0},{2,1},{3,2},{4,3},{5,4},{6,5},{7,6},{8,7},{9,8},{10,9},{11,1... | collective-permute-start | bytes 24584 | tf_op jit(solution)/shard_map/while/body/eval_jaxpr/ppermute | solution.py:23
  232.2 7.0 %collective-permute-start = (f32[1,32,64]{2,1,0:T(8,128)S(1)}, f32[1,32,64]{2,1,0:T(8,128)S(1)}, u32[]{:S(2)}, u32[]{:S(2)}) collective-permute-start(f32[1,32,64]{2,1,0:T(8,128)S(1)} %broadcast_select_fusion.4), channel_id=1, source_target_pairs={{1,0},{2,1},{3,2},{4,3},{5,4},{6,5},{7,6},{8,7},{9,8},{10,9},{11,1... | collective-permute-start | bytes 24584 | tf_op jit(solution)/shard_map/while/body/eval_jaxpr/ppermute | solution.py:23
  264.6 7.0 %collective-permute-start = (f32[1,32,64]{2,1,0:T(8,128)S(1)}, f32[1,32,64]{2,1,0:T(8,128)S(1)}, u32[]{:S(2)}, u32[]{:S(2)}) collective-permute-start(f32[1,32,64]{2,1,0:T(8,128)S(1)} %broadcast_select_fusion.4), channel_id=1, source_target_pairs={{1,0},{2,1},{3,2},{4,3},{5,4},{6,5},{7,6},{8,7},{9,8},{10,9},{11,1... | collective-permute-start | bytes 24584 | tf_op jit(solution)/shard_map/while/body/eval_jaxpr/ppermute | solution.py:23
  272.7 7.0 %collective-permute-start = (f32[1,32,64]{2,1,0:T(8,128)S(1)}, f32[1,32,64]{2,1,0:T(8,128)S(1)}, u32[]{:S(2)}, u32[]{:S(2)}) collective-permute-start(f32[1,32,64]{2,1,0:T(8,128)S(1)} %broadcast_select_fusion.4), channel_id=1, source_target_pairs={{1,0},{2,1},{3,2},{4,3},{5,4},{6,5},{7,6},{8,7},{9,8},{10,9},{11,1... | collective-permute-start | bytes 24584 | tf_op jit(solution)/shard_map/while/body/eval_jaxpr/ppermute | solution.py:23
  298.1 7.7 %collective-permute-start.20 = (f32[1,128,256]{1,2,0:T(8,128)S(1)}, f32[1,128,256]{1,2,0:T(8,128)S(1)}, u32[]{:S(2)}, u32[]{:S(2)}) collective-permute-start(f32[1,128,256]{1,2,0:T(8,128)S(1)} %get-tuple-element.180), channel_id=1, source_target_pairs={{1,0},{2,1},{3,2},{4,3},{5,4},{6,5},{7,6},{8,7},{9,8},{10,9},{11,1... | collective-permute-start | bytes 393224 | tf_op jit(solution)/shard_map/ppermute | solution.py:23
  317.6 7.7 %collective-permute-start.24 = (f32[1,128,256]{1,2,0:T(8,128)S(1)}, f32[1,128,256]{1,2,0:T(8,128)S(1)}, u32[]{:S(2)}, u32[]{:S(2)}) collective-permute-start(f32[1,128,256]{1,2,0:T(8,128)S(1)} %get-tuple-element.176), channel_id=1, source_target_pairs={{1,0},{2,1},{3,2},{4,3},{5,4},{6,5},{7,6},{8,7},{9,8},{10,9},{11,1... | collective-permute-start | bytes 393224 | tf_op jit(solution)/shard_map/ppermute | solution.py:23
  327.7 7.9 %collective-permute-start.26 = (f32[1,128,256]{1,2,0:T(8,128)S(1)}, f32[1,128,256]{1,2,0:T(8,128)S(1)}, u32[]{:S(2)}, u32[]{:S(2)}) collective-permute-start(f32[1,128,256]{1,2,0:T(8,128)S(1)} %get-tuple-element.174), channel_id=1, source_target_pairs={{1,0},{2,1},{3,2},{4,3},{5,4},{6,5},{7,6},{8,7},{9,8},{10,9},{11,1... | collective-permute-start | bytes 393224 | tf_op jit(solution)/shard_map/ppermute | solution.py:23
  329.6 7.2 %collective-permute-start.27 = (f32[1,128,256]{1,2,0:T(8,128)S(1)}, f32[1,128,256]{1,2,0:T(8,128)S(1)}, u32[]{:S(2)}, u32[]{:S(2)}) collective-permute-start(f32[1,128,256]{1,2,0:T(8,128)S(1)} %get-tuple-element.173), channel_id=1, source_target_pairs={{0,1},{1,2},{2,3},{3,4},{4,5},{5,6},{6,7},{7,8},{8,9},{9,10},{10,1... | collective-permute-start | bytes 393224 | tf_op jit(solution)/shard_map/ppermute | solution.py:22
  337.9 7.9 %collective-permute-start.28 = (f32[1,128,256]{1,2,0:T(8,128)S(1)}, f32[1,128,256]{1,2,0:T(8,128)S(1)}, u32[]{:S(2)}, u32[]{:S(2)}) collective-permute-start(f32[1,128,256]{1,2,0:T(8,128)S(1)} %get-tuple-element.172), channel_id=1, source_target_pairs={{1,0},{2,1},{3,2},{4,3},{5,4},{6,5},{7,6},{8,7},{9,8},{10,9},{11,1... | collective-permute-start | bytes 393224 | tf_op jit(solution)/shard_map/ppermute | solution.py:23
  339.9 7.2 %collective-permute-start.29 = (f32[1,128,256]{1,2,0:T(8,128)S(1)}, f32[1,128,256]{1,2,0:T(8,128)S(1)}, u32[]{:S(2)}, u32[]{:S(2)}) collective-permute-start(f32[1,128,256]{1,2,0:T(8,128)S(1)} %get-tuple-element.171), channel_id=1, source_target_pairs={{0,1},{1,2},{2,3},{3,4},{4,5},{5,6},{6,7},{7,8},{8,9},{9,10},{10,1... | collective-permute-start | bytes 393224 | tf_op jit(solution)/shard_map/ppermute | solution.py:22
  395.5 7.2 %collective-permute-start.30 = (f32[1,64,128]{2,1,0:T(8,128)S(1)}, f32[1,64,128]{2,1,0:T(8,128)S(1)}, u32[]{:S(2)}, u32[]{:S(2)}) collective-permute-start(f32[1,64,128]{2,1,0:T(8,128)S(1)} %get-tuple-element.194), channel_id=1, source_target_pairs={{1,0},{2,1},{3,2},{4,3},{5,4},{6,5},{7,6},{8,7},{9,8},{10,9},{11,1... | collective-permute-start | bytes 98312 | tf_op jit(solution)/shard_map/ppermute | solution.py:23
  404.0 8.0 %collective-permute-start.32 = (f32[1,64,128]{2,1,0:T(8,128)S(1)}, f32[1,64,128]{2,1,0:T(8,128)S(1)}, u32[]{:S(2)}, u32[]{:S(2)}) collective-permute-start(f32[1,64,128]{2,1,0:T(8,128)S(1)} %get-tuple-element.192), channel_id=1, source_target_pairs={{1,0},{2,1},{3,2},{4,3},{5,4},{6,5},{7,6},{8,7},{9,8},{10,9},{11,1... | collective-permute-start | bytes 98312 | tf_op jit(solution)/shard_map/ppermute | solution.py:23
  406.0 7.1 %collective-permute-start.33 = (f32[1,64,128]{2,1,0:T(8,128)S(1)}, f32[1,64,128]{2,1,0:T(8,128)S(1)}, u32[]{:S(2)}, u32[]{:S(2)}) collective-permute-start(f32[1,64,128]{2,1,0:T(8,128)S(1)} %get-tuple-element.191), channel_id=1, source_target_pairs={{0,1},{1,2},{2,3},{3,4},{4,5},{5,6},{6,7},{7,8},{8,9},{9,10},{10,1... | collective-permute-start | bytes 98312 | tf_op jit(solution)/shard_map/ppermute | solution.py:22
  418.7 7.2 %collective-permute-start.2 = (f32[1,32,64]{2,1,0:T(8,128)S(1)}, f32[1,32,64]{2,1,0:T(8,128)S(1)}, u32[]{:S(2)}, u32[]{:S(2)}) collective-permute-start(f32[1,32,64]{2,1,0:T(8,128)S(1)} %broadcast_select_fusion.5), channel_id=1, source_target_pairs={{1,0},{2,1},{3,2},{4,3},{5,4},{6,5},{7,6},{8,7},{9,8},{10,9},{11,1... | collective-permute-start | bytes 24584 | tf_op jit(solution)/shard_map/while/body/eval_jaxpr/ppermute | solution.py:23
  427.0 7.2 %collective-permute-start.2 = (f32[1,32,64]{2,1,0:T(8,128)S(1)}, f32[1,32,64]{2,1,0:T(8,128)S(1)}, u32[]{:S(2)}, u32[]{:S(2)}) collective-permute-start(f32[1,32,64]{2,1,0:T(8,128)S(1)} %broadcast_select_fusion.5), channel_id=1, source_target_pairs={{1,0},{2,1},{3,2},{4,3},{5,4},{6,5},{7,6},{8,7},{9,8},{10,9},{11,1... | collective-permute-start | bytes 24584 | tf_op jit(solution)/shard_map/while/body/eval_jaxpr/ppermute | solution.py:23
  435.3 7.1 %collective-permute-start.2 = (f32[1,32,64]{2,1,0:T(8,128)S(1)}, f32[1,32,64]{2,1,0:T(8,128)S(1)}, u32[]{:S(2)}, u32[]{:S(2)}) collective-permute-start(f32[1,32,64]{2,1,0:T(8,128)S(1)} %broadcast_select_fusion.5), channel_id=1, source_target_pairs={{1,0},{2,1},{3,2},{4,3},{5,4},{6,5},{7,6},{8,7},{9,8},{10,9},{11,1... | collective-permute-start | bytes 24584 | tf_op jit(solution)/shard_map/while/body/eval_jaxpr/ppermute | solution.py:23
  459.6 7.0 %collective-permute-start.2 = (f32[1,32,64]{2,1,0:T(8,128)S(1)}, f32[1,32,64]{2,1,0:T(8,128)S(1)}, u32[]{:S(2)}, u32[]{:S(2)}) collective-permute-start(f32[1,32,64]{2,1,0:T(8,128)S(1)} %broadcast_select_fusion.5), channel_id=1, source_target_pairs={{1,0},{2,1},{3,2},{4,3},{5,4},{6,5},{7,6},{8,7},{9,8},{10,9},{11,1... | collective-permute-start | bytes 24584 | tf_op jit(solution)/shard_map/while/body/eval_jaxpr/ppermute | solution.py:23
  467.7 7.0 %collective-permute-start.2 = (f32[1,32,64]{2,1,0:T(8,128)S(1)}, f32[1,32,64]{2,1,0:T(8,128)S(1)}, u32[]{:S(2)}, u32[]{:S(2)}) collective-permute-start(f32[1,32,64]{2,1,0:T(8,128)S(1)} %broadcast_select_fusion.5), channel_id=1, source_target_pairs={{1,0},{2,1},{3,2},{4,3},{5,4},{6,5},{7,6},{8,7},{9,8},{10,9},{11,1... | collective-permute-start | bytes 24584 | tf_op jit(solution)/shard_map/while/body/eval_jaxpr/ppermute | solution.py:23
  500.1 7.0 %collective-permute-start.2 = (f32[1,32,64]{2,1,0:T(8,128)S(1)}, f32[1,32,64]{2,1,0:T(8,128)S(1)}, u32[]{:S(2)}, u32[]{:S(2)}) collective-permute-start(f32[1,32,64]{2,1,0:T(8,128)S(1)} %broadcast_select_fusion.5), channel_id=1, source_target_pairs={{1,0},{2,1},{3,2},{4,3},{5,4},{6,5},{7,6},{8,7},{9,8},{10,9},{11,1... | collective-permute-start | bytes 24584 | tf_op jit(solution)/shard_map/while/body/eval_jaxpr/ppermute | solution.py:23
  540.7 7.0 %collective-permute-start.2 = (f32[1,32,64]{2,1,0:T(8,128)S(1)}, f32[1,32,64]{2,1,0:T(8,128)S(1)}, u32[]{:S(2)}, u32[]{:S(2)}) collective-permute-start(f32[1,32,64]{2,1,0:T(8,128)S(1)} %broadcast_select_fusion.5), channel_id=1, source_target_pairs={{1,0},{2,1},{3,2},{4,3},{5,4},{6,5},{7,6},{8,7},{9,8},{10,9},{11,1... | collective-permute-start | bytes 24584 | tf_op jit(solution)/shard_map/while/body/eval_jaxpr/ppermute | solution.py:23
  566.1 7.7 %collective-permute-start.38 = (f32[1,128,256]{1,2,0:T(8,128)S(1)}, f32[1,128,256]{1,2,0:T(8,128)S(1)}, u32[]{:S(2)}, u32[]{:S(2)}) collective-permute-start(f32[1,128,256]{1,2,0:T(8,128)S(1)} %get-tuple-element.170), channel_id=1, source_target_pairs={{1,0},{2,1},{3,2},{4,3},{5,4},{6,5},{7,6},{8,7},{9,8},{10,9},{11,1... | collective-permute-start | bytes 393224 | tf_op jit(solution)/shard_map/ppermute | solution.py:23
  585.5 7.7 %collective-permute-start.42 = (f32[1,128,256]{1,2,0:T(8,128)S(1)}, f32[1,128,256]{1,2,0:T(8,128)S(1)}, u32[]{:S(2)}, u32[]{:S(2)}) collective-permute-start(f32[1,128,256]{1,2,0:T(8,128)S(1)} %slice.873), channel_id=1, source_target_pairs={{1,0},{2,1},{3,2},{4,3},{5,4},{6,5},{7,6},{8,7},{9,8},{10,9},{11,1... | collective-permute-start | bytes 393224 | tf_op jit(solution)/shard_map/ppermute | solution.py:31
  (73 other events, 465.6 us)
where the time goes:
time: 604 us; the launch traced here: 595 us
  starting transfers between devices  354 us (59%)
  local copies, waits for them, and re-layouts  123 us (20%)
  other arithmetic  62.3 us (10%)
  waiting for transfers between devices  52.4 us (9%)
    ppermute x51, starting transfers between devices, extended(): before = lax.ppermute(last, axis, up)  254 us
    reshape x3, local copies, waits for them, and re-layouts, restrict(): field.reshape(sx // 2, 2, sy // 2, 2, sz // 2, 2).mean(axis=(1, 3, 5))  105 us
    ppermute x51, starting transfers between devices, extended(): after = lax.ppermute(initial, axis, down)  98 us
    ppermute x51, waiting for transfers between devices, extended(): before = lax.ppermute(last, axis, up)  43.1 us
    reduce_sum x8, other arithmetic, restrict(): field.reshape(sx // 2, 2, sy // 2, 2, sz // 2, 2).mean(axis=(1, 3, 5))  42.8 us
  transfers between devices with their start and end apart: 103, of which 55 were waited for; matrix products, arithmetic and copies ran while one was open for 9% of the time, Pallas kernels for 0%

commit v1 on v0

v1 whole, which is shorter than its diff:
```python
import functools

import jax
import jax.numpy as jnp
from jax import lax
from jax.experimental import pallas as pl
from jax.experimental.pallas import tpu as pltpu
from jax.sharding import PartitionSpec as P

SWEEPS = 2
COARSE = 16
CYCLES = 2
DAMPING = 0.8
KEEP = 1.0 - DAMPING
RATE = 0.004
MESH = pl.DeviceIdType.MESH
PAD = 8
CHUNK = 32


def dot(a, b):
    return lax.dot(a, b, precision=lax.Precision.HIGHEST, preferred_element_type=jnp.float32)


def pick(shape, row_of, column_of):
    r = lax.broadcasted_iota(jnp.int32, shape, 0)
    c = lax.broadcasted_iota(jnp.int32, shape, 1)
    return jnp.where(row_of(r) == column_of(c), 1.0, 0.0).astype(jnp.float32)


def z_sides(x):
    last = x.shape[1] - 1
    lane = lax.broadcasted_iota(jnp.int32, x.shape, 1)
    before = jnp.where(lane == 0, 0.0, pltpu.roll(x, 1, 1))
    return before + jnp.where(lane == last, 0.0, pltpu.roll(x, last, 1))


def y_sides(x):
    last = x.shape[0] - 1
    row = lax.broadcasted_iota(jnp.int32, x.shape, 0)
    before = jnp.where(row == 0, 0.0, pltpu.roll(x, 1, 0))
    return before + jnp.where(row == last, 0.0, pltpu.roll(x, last, 0))


def kernel(n, f_ref, counts_ref, out_ref, ahead_ref, va, vb, c_ref, d_ref, halo, quarter, rs,
           cm, rm, e2, ea, eb, qown, gc, gr, xa, xb, fsend, frecv, gsend, grecv):
    me = lax.axis_index("gx")
    ny, nz = f_ref.shape[1:]
    my, mz = ny // 2, nz // 2
    cy, cz = my // 4, mz
    rows = pl.ds(PAD, ny)

    for ref in (va, vb):
        for p in range(ref.shape[0]):
            ref[p, pl.ds(0, PAD), :] = jnp.zeros((PAD, nz), jnp.float32)
            ref[p, pl.ds(PAD + ny, PAD), :] = jnp.zeros((PAD, nz), jnp.float32)
    cm[...] = jnp.zeros_like(cm)
    rm[...] = jnp.zeros_like(rm)
    e2[...] = jnp.zeros_like(e2)
    for ref in (xa, xb):
        for p in (0, 1, n + 2, n + 3):
            ref[p] = jnp.zeros((cy, cz), jnp.float32)

    @pl.when(me == 0)
    def _():
        for k in range(halo.shape[0]):
            halo[k, 0] = jnp.zeros((ny, nz), jnp.float32)
        for k in range(CYCLES):
            quarter[k, 0] = jnp.zeros((my, mz), jnp.float32)

    @pl.when(me == n - 1)
    def _():
        for k in range(halo.shape[0]):
            halo[k, 1] = jnp.zeros((ny, nz), jnp.float32)
        for k in range(CYCLES):
            quarter[k, 1] = jnp.zeros((my, mz), jnp.float32)

    barrier = pltpu.get_barrier_semaphore()

    def greet(k, _):
        pl.semaphore_signal(barrier, inc=1, device_id={"gx": lax.rem(me + k, n)}, device_id_type=MESH)
        return 0

    lax.fori_loop(1, n, greet, 0)

    used = [0]

    class Transfer:
        def __init__(self, src, dst, dist):
            self.dist, self.src, self.dst, self.j = dist, src, dst, used[0]
            used[0] += 1

        def copy(self):
            return pltpu.make_async_remote_copy(
                src_ref=self.src, dst_ref=self.dst, send_sem=fsend.at[self.j],
                recv_sem=frecv.at[self.j], device_id={"gx": me + self.dist}, device_id_type=MESH)

        def inside(self, sign):
            return me < n - self.dist * sign if self.dist * sign > 0 else me >= -self.dist * sign

        def start(self):
            @pl.when(self.inside(1))
            def _():
                self.copy().start()
            return self

        def arrived(self):
            @pl.when(self.inside(-1))
            def _():
                self.copy().wait_recv()

        def sent(self):
            @pl.when(self.inside(1))
            def _():
                self.copy().wait_send()

        def wait(self):
            self.arrived()
            self.sent()

    def gather_copy(g, ref, k, peer, owner):
        return pltpu.make_async_remote_copy(
            src_ref=ref.at[owner], dst_ref=ref.at[owner], send_sem=gsend.at[g, k],
            recv_sem=grecv.at[g, k], device_id={"gx": peer}, device_id_type=MESH)

    def gather_start(g, ref):
        def body(k, _):
            gather_copy(g, ref, k, lax.rem(me + k, n), me).start()
            return 0
        lax.fori_loop(1, n, body, 0)

    def gather_wait(g, ref):
        def body(k, _):
            c = gather_copy(g, ref, k, lax.rem(me + k, n), lax.rem(me + n - k, n))
            c.wait_recv()
            c.wait_send()
            return 0
        lax.fori_loop(1, n, body, 0)

    def halves(r, c):
        return r // 2, c // 2

    ry_f = pick((my, ny), lambda r: r, lambda c: c // 2)
    rz_f = pick((nz, mz), lambda r: r // 2, lambda c: c)
    py_f = pick((ny, my), lambda r: r // 2, lambda c: c)
    pz_f = pick((mz, nz), lambda r: r, lambda c: c // 2)
    half = mz // 2
    ry_m = [pick((cy, my), lambda r, o=o: 2 * r + o, lambda c: c // 2) for o in (0, 1)]
    rz_m = [pick((mz, cz), lambda r, o=o: r // 2 + o * half, lambda c: c) for o in (0, 1)]
    py_m = [pick((my, cy), lambda r: r // 2, lambda c, o=o: 2 * c + o) for o in (0, 1)]
    pz_m = [pick((cz, mz), lambda r: r, lambda c, o=o: c // 2 + o * half) for o in (0, 1)]

    def sum_fine(x):
        return dot(dot(ry_f, x), rz_f)

    def spread_fine(x):
        return dot(dot(py_f, x), pz_f)

    def sum_mid(x):
        return dot(dot(ry_m[0], x), rz_m[0]) + dot(dot(ry_m[1], x), rz_m[1])

    def spread_mid(x):
        return dot(py_m[0], dot(x, pz_m[0])) + dot(py_m[1], dot(x, pz_m[1]))

    def chunks(body):
        def step(i, _):
            body(pl.multiple_of(i * CHUNK, CHUNK))
            return 0
        lax.fori_loop(0, ny // CHUNK, step, 0)

    def prepare(p):
        def body(r):
            screen = RATE * counts_ref[p, pl.ds(r, CHUNK), :].astype(jnp.float32)
            d = 6.0 + screen
            c = DAMPING / d
            d_ref[p, pl.ds(r, CHUNK), :] = d
            c_ref[p, pl.ds(r, CHUNK), :] = c
            va[p, pl.ds(r + PAD, CHUNK), :] = c * f_ref[p, pl.ds(r, CHUNK), :]
        chunks(body)

    state = {"slot": 0}

    def exchange(v):
        k = state["slot"]
        state["slot"] += 1
        up = Transfer(v.at[3, rows, :], halo.at[k, 0], 1)
        down = Transfer(v.at[0, rows, :], halo.at[k, 1], -1)
        return k, up, down

    def neighbours(v, p, r, low, high):
        win = v[p, pl.ds(r, CHUNK + 2 * PAD), :]
        x = win[PAD:PAD + CHUNK]
        nb = win[PAD - 1:PAD - 1 + CHUNK] + win[PAD + 1:PAD + 1 + CHUNK] + z_sides(x)
        nb += v[p - 1, pl.ds(r + PAD, CHUNK), :] if p > 0 else low
        nb += v[p + 1, pl.ds(r + PAD, CHUNK), :] if p < 3 else high
        return x, nb

    def relax(dst, v, k, planes):
        def body(r):
            for p in planes:
                x, nb = neighbours(v, p, r, halo[k, 0, pl.ds(r, CHUNK), :], halo[k, 1, pl.ds(r, CHUNK), :])
                dst[p, pl.ds(r + PAD, CHUNK), :] = KEEP * x + c_ref[p, pl.ds(r, CHUNK), :] * (
                    f_ref[p, pl.ds(r, CHUNK), :] + nb)
        chunks(body)

    def relax_exchanged(dst, v, k, up, down):
        relax(dst, v, k, (1, 2))
        up.wait()
        down.wait()
        relax(dst, v, k, (0, 3))

    for p in (0, 3):
        prepare(p)
    pl.semaphore_wait(barrier, n - 1)
    first = exchange(va)
    first[1].start()
    first[2].start()
    for p in (1, 2):
        prepare(p)

    mid_screen = []
    for m in range(2):
        s = d_ref[2 * m] + d_ref[2 * m + 1] - 12.0
        mid_screen.append(0.125 * sum_fine(s))
        cm[2 + m] = DAMPING / (1.5 + mid_screen[m])
    cm_up = Transfer(cm.at[pl.ds(2, 2)], cm.at[pl.ds(0, 2)], 1).start()
    cm_down = Transfer(cm.at[pl.ds(2, 2)], cm.at[pl.ds(4, 2)], -1).start()
    gc[me] = DAMPING / (0.375 + 0.125 * sum_mid(mid_screen[0] + mid_screen[1]))
    gather_start(CYCLES, gc)

    lane = lax.broadcasted_iota(jnp.int32, (cy, cz), 1)
    row = lax.broadcasted_iota(jnp.int32, (cy, cz), 0)
    even = lane < half
    z_first, z_last = lax.rem(lane, half) == 0, lax.rem(lane, half) == half - 1

    def coarse_sides(x):
        w = pltpu.roll(x, half, 1)
        before = jnp.where(row == 0, 0.0, pltpu.roll(w, 1, 0))
        after = jnp.where(row == cy - 1, 0.0, pltpu.roll(w, cy - 1, 0))
        nb = w + jnp.where(even, before, after)
        nb += jnp.where(z_first, 0.0, pltpu.roll(x, 1, 1))
        return nb + jnp.where(z_last, 0.0, pltpu.roll(x, cz - 1, 1))

    GROUP = 4

    def coarse_sweep(dst, src):
        def body(g, _):
            for j in range(GROUP):
                q = g * GROUP + j
                x = src[q + 2]
                nb = coarse_sides(x) + src[q + 1] + src[q + 3]
                dst[q + 2] = KEEP * x + gr[CYCLES, q] + gc[q] * (0.0625 * nb)
            return 0
        lax.fori_loop(0, n // GROUP, body, 0)

    def vcycle(cycle, begun, spare, field):
        k, up, down = begun
        relax_exchanged(spare, field, k, up, down)
        quarters = []
        for side, p, dist in ((0, 3, 1), (1, 0, -1)):
            qown[cycle, side] = 0.5 * 0.25 * sum_fine(spare[p, rows, :])
            quarters.append(Transfer(qown.at[cycle, side], quarter.at[cycle, side], dist).start())
        kept, up, down = exchange(spare)
        up.start()
        down.start()

        for m in range(2):
            def body(r, m=m):
                total = None
                for p in (2 * m, 2 * m + 1):
                    x, nb = neighbours(spare, p, r, 0.0, 0.0)
                    res = f_ref[p, pl.ds(r, CHUNK), :] - d_ref[p, pl.ds(r, CHUNK), :] * x + nb
                    total = res if total is None else total + res
                rs[m, pl.ds(r, CHUNK), :] = total
            chunks(body)
        for m in range(2):
            rm[cycle, 2 + m] = 0.125 * sum_fine(rs[m])
        for t in quarters:
            t.wait()
        rm[cycle, 2] += quarter[cycle, 0]
        rm[cycle, 3] += quarter[cycle, 1]
        rm_up = Transfer(rm.at[cycle, pl.ds(2, 2)], rm.at[cycle, pl.ds(0, 2)], 1).start()
        rm_down = Transfer(rm.at[cycle, pl.ds(2, 2)], rm.at[cycle, pl.ds(4, 2)], -1).start()
        if cycle == 0:
            cm_up.wait()
            cm_down.wait()
        rm_up.wait()
        rm_down.wait()
        for q in range(6):
            ea[q + 1] = cm[q] * rm[cycle, q]

        def mid_relax(dst, src, m):
            x = src[m + 3]
            nb = y_sides(x) + z_sides(x) + src[m + 2] + src[m + 4]
            dst[m + 3] = KEEP * x + cm[m + 2] * (rm[cycle, m + 2] + 0.25 * nb)

        for m in range(-1, 3):
            mid_relax(e2.at[cycle], ea, m)
        wide = [Transfer(e2.at[cycle, a], e2.at[cycle, b], dist).start()
                for a, b, dist in ((3, 1, 1), (4, 6, -1), (4, 0, 2), (3, 7, -2))]
        total = 0.0
        for m in range(2):
            x = e2[cycle, m + 3]
            nb = y_sides(x) + z_sides(x) + e2[cycle, m + 2] + e2[cycle, m + 4]
            total += rm[cycle, m + 2] - DAMPING / cm[m + 2] * x + 0.25 * nb
        gr[cycle, me] = 0.125 * sum_mid(total)
        gather_start(cycle, gr.at[cycle])
        if cycle == 0:
            gather_wait(CYCLES, gc)
        gather_wait(cycle, gr.at[cycle])

        def begin(q, _):
            g = gc[q] * gr[cycle, q]
            gr[CYCLES, q] = g
            xa[q + 2] = g
            return 0

        lax.fori_loop(0, n, begin, 0)

        def twice(_, c):
            coarse_sweep(xb, xa)
            coarse_sweep(xa, xb)
            return c

        lax.fori_loop(0, (COARSE - 1) // 2, twice, 0)
        coarse_sweep(xb, xa)

        for t in wide:
            t.wait()
        for j in range(5):
            e = spread_mid(xb[me + j])
            for m in (2 * (j - 2), 2 * (j - 2) + 1):
                if -3 <= m <= 4:
                    ea[m + 3] = e2[cycle, m + 3] + e
        for m in range(-2, 4):
            mid_relax(eb, ea, m)
        for m in range(-1, 3):
            mid_relax(ea, eb, m)
        up.wait()
        down.wait()
        for m in range(-1, 3):
            e = spread_fine(ea[m + 3])
            if m == -1:
                @pl.when(me > 0)
                def _():
                    halo[kept, 0] += e
            elif m == 2:
                @pl.when(me < n - 1)
                def _():
                    halo[kept, 1] += e
            else:
                for p in (2 * m, 2 * m + 1):
                    spare[p, rows, :] += e
        for p_pair in ((0, 3), (1, 2)):
            relax(field, spare, kept, p_pair)
            if p_pair == (0, 3):
                post = exchange(field)
                post[1].start()
                post[2].start()
        relax_exchanged(spare, field, *post)
        return spare, field

    done, spare = vcycle(0, first, vb, va)
    again = exchange(done)
    again[1].start()
    again[2].start()
    relax_exchanged(spare, done, *again)
    begun = exchange(spare)
    begun[1].start()
    begun[2].start()
    done, spare = vcycle(1, begun, done, spare)
    k = state["slot"]
    last = Transfer(done.at[0, rows, :], halo.at[k, 1], -1).start()
    for p in range(4):
        out_ref[p] = done[p, rows, :]
    last.wait()
    ahead_ref[0] = halo[k, 1]


def shards(n, cotangent, counts):
    nx, ny, nz = cotangent.shape
    f32 = jnp.float32
    my, mz = ny // 2, nz // 2
    cy, cz = my // 4, mz
    vmem = pl.BlockSpec(memory_space=pltpu.VMEM)
    slots = 8
    multiplier, following = pl.pallas_call(
        functools.partial(kernel, n),
        out_shape=(jax.ShapeDtypeStruct((nx, ny, nz), f32), jax.ShapeDtypeStruct((1, ny, nz), f32)),
        in_specs=[vmem, vmem],
        out_specs=(vmem, vmem),
        scratch_shapes=[
            pltpu.VMEM((nx, ny + 2 * PAD, nz), f32),
            pltpu.VMEM((nx, ny + 2 * PAD, nz), f32),
            pltpu.VMEM((nx, ny, nz), f32),
            pltpu.VMEM((nx, ny, nz), f32),
            pltpu.VMEM((slots, 2, ny, nz), f32),
            pltpu.VMEM((CYCLES, 2, my, mz), f32),
            pltpu.VMEM((2, ny, nz), f32),
            pltpu.VMEM((6, my, mz), f32),
            pltpu.VMEM((CYCLES, 6, my, mz), f32),
            pltpu.VMEM((CYCLES, 8, my, mz), f32),
            pltpu.VMEM((8, my, mz), f32),
            pltpu.VMEM((8, my, mz), f32),
            pltpu.VMEM((CYCLES, 2, my, mz), f32),
            pltpu.VMEM((n, cy, cz), f32),
            pltpu.VMEM((CYCLES + 1, n, cy, cz), f32),
            pltpu.VMEM((n + 4, cy, cz), f32),
            pltpu.VMEM((n + 4, cy, cz), f32),
            pltpu.SemaphoreType.DMA((40,)),
            pltpu.SemaphoreType.DMA((40,)),
            pltpu.SemaphoreType.DMA((CYCLES + 1, n)),
            pltpu.SemaphoreType.DMA((CYCLES + 1, n)),
        ],
        compiler_params=pltpu.CompilerParams(
            collective_id=0, has_side_effects=True, vmem_limit_bytes=40 * 1024 * 1024),
    )(cotangent, counts)
    ahead_x = jnp.concatenate([multiplier[1:], following], axis=0)
    ahead_y = jnp.pad(multiplier[:, 1:], ((0, 0), (0, 1), (0, 0)))
    ahead_z = jnp.pad(multiplier[:, :, 1:], ((0, 0), (0, 0), (0, 1)))
    normal_grad = jnp.stack([multiplier - ahead_x, multiplier - ahead_y, multiplier - ahead_z])
    return (multiplier, normal_grad)


def solution(mesh):
    split = P(("scene", "gx"), None, None)
    return jax.shard_map(
        functools.partial(shards, mesh.shape["gx"]),
        mesh=mesh,
        in_specs=(split, split),
        out_specs=(split, P(None, ("scene", "gx"), None, None)),
        check_vma=False,
    )
```

time: 604 us -> 86.8 us (0.14); the launches traced: 595 us -> 86.6 us
  starting transfers between devices: 354 us -> 0 us
  local copies, waits for them, and re-layouts: 123 us -> 3.13 us
  Pallas kernels: 0 us -> 81.4 us
  other arithmetic: 62.3 us -> 1.39 us
  waiting for transfers between devices: 52.4 us -> 0 us
    ppermute x103 -> x0, starting transfers between devices: 354 us -> none  [the longest x51 254 us: extended(): before = lax.ppermute(last, axis, up)]
    reshape x5 -> x0, local copies, waits for them, and re-layouts: 105 us -> none  [the longest x3 105 us: restrict(): field.reshape(sx // 2, 2, sy // 2, 2, sz // 2, 2).mean(axis=(1, 3, 5))]
    pallas_call x0 -> x1, Pallas kernels: none -> 81.4 us  [shards(): pl.pallas_call(functools.partial(kernel, n), out_shape=(jax.ShapeDtypeStr...]
    ppermute x103 -> x0, waiting for transfers between devices: 52.4 us -> none  [the longest x51 43.1 us: extended(): before = lax.ppermute(last, axis, up)]
    reduce_sum x8 -> x0, other arithmetic: 42.8 us -> none  [restrict(): field.reshape(sx // 2, 2, sy // 2, 2, sz // 2, 2).mean(axis=(1, 3, 5))]
    reduce_sum x3 -> x0, local copies, waits for them, and re-layouts: 10.4 us -> none  [restrict(): field.reshape(sx // 2, 2, sy // 2, 2, sz // 2, 2).mean(axis=(1, 3, 5))]
    concatenate x51 -> x0, other arithmetic: 8.9 us -> none  [extended(): array = jnp.concatenate([before, array, after], axis=dim)]
    add x48 -> x0, other arithmetic: 7.61 us -> none  [the longest x6 3.7 us: smooth_fine(): field + damping * (source - apply_fine(field, screen_fine)) / (6.0 + scre...]
  transfers between devices with their start and end apart: 103 -> 0, of which waited for: 55 -> 0; matrix products, arithmetic and copies ran while one was open for 9% -> 0% of each run, Pallas kernels for 0% -> 0%
where the time goes in v1:
time: 86.8 us; the launch traced here: 86.6 us
  Pallas kernels  81.4 us (94%)
  local copies, waits for them, and re-layouts  3.13 us (4%)
  other arithmetic  1.39 us (2%)
    pallas_call x1, Pallas kernels, shards(): pl.pallas_call(functools.partial(kernel, n), out_shape=(jax.ShapeDtypeStr...  81.4 us
    unnamed x5, local copies, waits for them, and re-layouts  2.87 us

profile of v1, /device:TPU:1, one launch (start us, length us, event | category | flops | bytes accessed | tf_op | source)
XLA Modules:
  0.0 86.6 jit_solution(13848242636949421806)
XLA Ops:
  0.6 0.0 copy-start
  0.6 1.0 %copy-done = f32[4,128,256]{2,1,0:T(8,128)S(1)} copy-done((f32[4,128,256]{2,1,0:T(8,128)S(1)}, f32[4,128,256]{2,1,0:T(8,128)}, u32[]{:S(2)}) %copy-start) | copy-done | bytes 524312
  1.7 0.0 copy-start.1
  1.7 1.0 %copy-done.1 = s32[4,128,256]{2,1,0:T(8,128)S(1)} copy-done((s32[4,128,256]{2,1,0:T(8,128)S(1)}, s32[4,128,256]{2,1,0:T(8,128)}, u32[]{:S(2)}) %copy-start.1) | copy-done | bytes 524312
  2.7 81.4 %shard_map.41 = (f32[4,128,256]{2,1,0:T(8,128)S(1)}, f32[1,128,256]{2,1,0:T(8,128)S(1)}) custom-call(f32[4,128,256]{2,1,0:T(8,128)S(1)} %copy-done, s32[4,128,256]{2,1,0:T(8,128)S(1)} %copy-done.1), custom_call_target="tpu_custom_call" | custom-call | tf_op jit(solution)/shard_map/pallas_call | solution.py:387
  84.2 0.2 slice.11
  84.4 0.1 fusion
  84.6 1.2 %pad_maximum_fusion = f32[3,4,128,256]{3,2,1,0:T(8,128)} fusion(f32[1,4,128,256]{3,2,1,0:T(8,128)S(1)} %get-tuple-element.7, f32[1,4,128,256]{3,2,1,0:T(8,128)S(1)} %get-tuple-element.8, f32[1,4,128,256]{3,2,1,0:T(8,128)S(1)} %get-tuple-element.6), kind=kLoop, calls=%fused_computation | loop fusion | flops 786432 | bytes 3145728 | tf_op jit(solution)/shard_map/stack | solution.py:421
  85.8 0.8 copy.5
  (2 shorter events, 0.1 us)
Async XLA Ops:
  0.6 1.0 %copy-start = (f32[4,128,256]{2,1,0:T(8,128)S(1)}, f32[4,128,256]{2,1,0:T(8,128)}, u32[]{:S(2)}) copy-start(f32[4,128,256]{2,1,0:T(8,128)} %f_ref.1) | copy-start | bytes 1572868
  1.7 1.0 %copy-start.1 = (s32[4,128,256]{2,1,0:T(8,128)S(1)}, s32[4,128,256]{2,1,0:T(8,128)}, u32[]{:S(2)}) copy-start(s32[4,128,256]{2,1,0:T(8,128)} %counts_ref.1) | copy-start | bytes 1572868

commit v2 on v1

--- a/solution.py
+++ b/solution.py
@@ -19,13 +19,13 @@
 
 
 def dot(a, b):
-    return lax.dot(a, b, precision=lax.Precision.HIGHEST, preferred_element_type=jnp.float32)
+    return lax.dot(a, b, preferred_element_type=jnp.float32)
 
 
 def pick(shape, row_of, column_of):
     r = lax.broadcasted_iota(jnp.int32, shape, 0)
     c = lax.broadcasted_iota(jnp.int32, shape, 1)
-    return jnp.where(row_of(r) == column_of(c), 1.0, 0.0).astype(jnp.float32)
+    return jnp.where(row_of(r) == column_of(c), 1.0, 0.0).astype(jnp.bfloat16)
 
 
 def z_sides(x):
@@ -42,38 +42,61 @@
     return before + jnp.where(row == last, 0.0, pltpu.roll(x, last, 0))
 
 
-def kernel(n, f_ref, counts_ref, out_ref, ahead_ref, va, vb, c_ref, d_ref, halo, quarter, rs,
-           cm, rm, e2, ea, eb, qown, gc, gr, xa, xb, fsend, frecv, gsend, grecv):
+def split(x):
+    high = x.astype(jnp.bfloat16)
+    return high, (x - high.astype(jnp.float32)).astype(jnp.bfloat16)
+
+
+def times(x, matrix):
+    high, low = split(x)
+    return dot(high, matrix) + dot(low, matrix)
+
+
+def timed(matrix, x):
+    high, low = split(x)
+    return dot(matrix, high) + dot(matrix, low)
+
+
+def kernel(n, f_hbm, counts_hbm, out_ref, ahead_ref, f_ref, counts_ref, va, vb, vd, ve, c_ref, d_ref, last,
+           quarter, rs, cm, rm, e2, ea, eb, qown, gc, gr, xa, xb, lsem, fsend, frecv, gsend, grecv):
     me = lax.axis_index("gx")
-    ny, nz = f_ref.shape[1:]
+    ny, nz = f_hbm.shape[1:]
     my, mz = ny // 2, nz // 2
     cy, cz = my // 4, mz
     rows = pl.ds(PAD, ny)
 
-    for ref in (va, vb):
+    local = [pltpu.make_async_copy(f_hbm, f_ref.at[pl.ds(1, 4)], lsem.at[0]),
+             pltpu.make_async_copy(counts_hbm, counts_ref.at[pl.ds(1, 4)], lsem.at[1])]
+    for copy in local:
+        copy.start()
+
+    for ref in (va, vb, vd, ve):
         for p in range(ref.shape[0]):
             ref[p, pl.ds(0, PAD), :] = jnp.zeros((PAD, nz), jnp.float32)
             ref[p, pl.ds(PAD + ny, PAD), :] = jnp.zeros((PAD, nz), jnp.float32)
     cm[...] = jnp.zeros_like(cm)
     rm[...] = jnp.zeros_like(rm)
     e2[...] = jnp.zeros_like(e2)
+    quarter[...] = jnp.zeros_like(quarter)
     for ref in (xa, xb):
         for p in (0, 1, n + 2, n + 3):
             ref[p] = jnp.zeros((cy, cz), jnp.float32)
 
+    def clear(side):
+        for ref in (vb, vd, ve):
+            for p in (6 * side, 6 * side + 1):
+                ref[p, rows, :] = jnp.zeros((ny, nz), jnp.float32)
+        f_ref[5 * side] = jnp.zeros((ny, nz), jnp.float32)
+        counts_ref[5 * side] = jnp.zeros((ny, nz), jnp.int32)
+
     @pl.when(me == 0)
     def _():
-        for k in range(halo.shape[0]):
-            halo[k, 0] = jnp.zeros((ny, nz), jnp.float32)
-        for k in range(CYCLES):
-            quarter[k, 0] = jnp.zeros((my, mz), jnp.float32)
+        clear(0)
 
     @pl.when(me == n - 1)
     def _():
-        for k in range(halo.shape[0]):
-            halo[k, 1] = jnp.zeros((ny, nz), jnp.float32)
-        for k in range(CYCLES):
-            quarter[k, 1] = jnp.zeros((my, mz), jnp.float32)
+        clear(1)
+        last[...] = jnp.zeros_like(last)
 
     barrier = pltpu.get_barrier_semaphore()
 
@@ -136,9 +159,6 @@
             c.wait_send()
             return 0
         lax.fori_loop(1, n, body, 0)
-
-    def halves(r, c):
-        return r // 2, c // 2
 
     ry_f = pick((my, ny), lambda r: r, lambda c: c // 2)
     rz_f = pick((nz, mz), lambda r: r // 2, lambda c: c)
@@ -151,16 +171,16 @@
     pz_m = [pick((cz, mz), lambda r: r, lambda c, o=o: c // 2 + o * half) for o in (0, 1)]
 
     def sum_fine(x):
-        return dot(dot(ry_f, x), rz_f)
+        return times(timed(ry_f, x), rz_f)
 
     def spread_fine(x):
-        return dot(dot(py_f, x), pz_f)
+        return times(timed(py_f, x), pz_f)
 
     def sum_mid(x):
-        return dot(dot(ry_m[0], x), rz_m[0]) + dot(dot(ry_m[1], x), rz_m[1])
+        return times(timed(ry_m[0], x), rz_m[0]) + times(timed(ry_m[1], x), rz_m[1])
 
     def spread_mid(x):
-        return dot(py_m[0], dot(x, pz_m[0])) + dot(py_m[1], dot(x, pz_m[1]))
+        return timed(py_m[0], times(x, pz_m[0])) + timed(py_m[1], times(x, pz_m[1]))
 
     def chunks(body):
         def step(i, _):
@@ -168,55 +188,56 @@
             return 0
         lax.fori_loop(0, ny // CHUNK, step, 0)
 
-    def prepare(p):
+    below, above = jnp.where(me > 0, DAMPING, 0.0), jnp.where(me < n - 1, DAMPING, 0.0)
+
+    def prepare(planes):
         def body(r):
-            screen = RATE * counts_ref[p, pl.ds(r, CHUNK), :].astype(jnp.float32)
-            d = 6.0 + screen
-            c = DAMPING / d
-            d_ref[p, pl.ds(r, CHUNK), :] = d
-            c_ref[p, pl.ds(r, CHUNK), :] = c
-            va[p, pl.ds(r + PAD, CHUNK), :] = c * f_ref[p, pl.ds(r, CHUNK), :]
+            at = pl.ds(r, CHUNK)
+            for p in planes:
+                d = 6.0 + RATE * counts_ref[p + 1, at, :].astype(jnp.float32)
+                c = (below if p < 0 else above if p > 3 else DAMPING) / d
+                if 0 <= p < 4:
+                    d_ref[p, at, :] = d
+                c_ref[p + 1, at, :] = c
+                va[p + 2, pl.ds(r + PAD, CHUNK), :] = c * f_ref[p + 1, at, :]
         chunks(body)
 
-    state = {"slot": 0}
-
-    def exchange(v):
-        k = state["slot"]
-        state["slot"] += 1
-        up = Transfer(v.at[3, rows, :], halo.at[k, 0], 1)
-        down = Transfer(v.at[0, rows, :], halo.at[k, 1], -1)
-        return k, up, down
-
-    def neighbours(v, p, r, low, high):
-        win = v[p, pl.ds(r, CHUNK + 2 * PAD), :]
+    def neighbours(v, p, r, low=None, high=None):
+        at = pl.ds(r + PAD, CHUNK)
+        win = v[p + 2, pl.ds(r, CHUNK + 2 * PAD), :]
         x = win[PAD:PAD + CHUNK]
         nb = win[PAD - 1:PAD - 1 + CHUNK] + win[PAD + 1:PAD + 1 + CHUNK] + z_sides(x)
-        nb += v[p - 1, pl.ds(r + PAD, CHUNK), :] if p > 0 else low
-        nb += v[p + 1, pl.ds(r + PAD, CHUNK), :] if p < 3 else high
+        for q, given in ((p - 1, low), (p + 1, high)):
+            if given is None:
+                nb += v[q + 2, at, :]
+            elif given is not False:
+                nb += given[0, pl.ds(r, CHUNK), :]
         return x, nb
 
-    def relax(dst, v, k, planes):
+    def relax(dst, v, planes, high=None, raw=False):
         def body(r):
+            at = pl.ds(r, CHUNK)
             for p in planes:
-                x, nb = neighbours(v, p, r, halo[k, 0, pl.ds(r, CHUNK), :], halo[k, 1, pl.ds(r, CHUNK), :])
-                dst[p, pl.ds(r + PAD, CHUNK), :] = KEEP * x + c_ref[p, pl.ds(r, CHUNK), :] * (
-                    f_ref[p, pl.ds(r, CHUNK), :] + nb)
+                x, nb = neighbours(v, p, r, None, high)
+                new = KEEP * x + c_ref[p + 1, at, :] * (f_ref[p + 1, at, :] + nb)
+                if raw:
+                    dst[p, at, :] = new
+                else:
+                    dst[p + 2, pl.ds(r + PAD, CHUNK), :] = new
         chunks(body)
 
-    def relax_exchanged(dst, v, k, up, down):
-        relax(dst, v, k, (1, 2))
-        up.wait()
-        down.wait()
-        relax(dst, v, k, (0, 3))
-
-    for p in (0, 3):
-        prepare(p)
+    def share(v):
+        return [Transfer(v.at[pl.ds(4, 2), rows, :], v.at[pl.ds(0, 2), rows, :], 1).start(),
+                Transfer(v.at[pl.ds(2, 2), rows, :], v.at[pl.ds(6, 2), rows, :], -1).start()]
+
     pl.semaphore_wait(barrier, n - 1)
-    first = exchange(va)
-    first[1].start()
-    first[2].start()
-    for p in (1, 2):
-        prepare(p)
+    first = []
+    for src, ref in ((counts_hbm, counts_ref), (f_hbm, f_ref)):
+        first.append(Transfer(src.at[3], ref.at[0], 1).start())
+        first.append(Transfer(src.at[0], ref.at[5], -1).start())
+    for copy in local:
+        copy.wait()
+    prepare((0, 1, 2, 3))
 
     mid_screen = []
     for m in range(2):
@@ -241,7 +262,7 @@
         nb += jnp.where(z_first, 0.0, pltpu.roll(x, 1, 1))
         return nb + jnp.where(z_last, 0.0, pltpu.roll(x, cz - 1, 1))
 
-    GROUP = 4
+    GROUP = 16 if n % 16 == 0 else 4
 
     def coarse_sweep(dst, src):
         def body(g, _):
@@ -253,39 +274,36 @@
             return 0
         lax.fori_loop(0, n // GROUP, body, 0)
 
-    def vcycle(cycle, begun, spare, field):
-        k, up, down = begun
-        relax_exchanged(spare, field, k, up, down)
-        quarters = []
+    def vcycle(cycle, v):
+        swaps = []
         for side, p, dist in ((0, 3, 1), (1, 0, -1)):
-            qown[cycle, side] = 0.5 * 0.25 * sum_fine(spare[p, rows, :])
-            quarters.append(Transfer(qown.at[cycle, side], quarter.at[cycle, side], dist).start())
-        kept, up, down = exchange(spare)
-        up.start()
-        down.start()
-
+            qown[cycle, side] = 0.5 * 0.25 * sum_fine(v[p + 2, rows, :])
+            for far in (1, 2):
+                swaps.append(Transfer(qown.at[cycle, side], quarter.at[cycle, far - 1, side], far * dist).start())
         for m in range(2):
             def body(r, m=m):
                 total = None
                 for p in (2 * m, 2 * m + 1):
-                    x, nb = neighbours(spare, p, r, 0.0, 0.0)
-                    res = f_ref[p, pl.ds(r, CHUNK), :] - d_ref[p, pl.ds(r, CHUNK), :] * x + nb
+                    x, nb = neighbours(v, p, r, False if p == 0 else None, False if p == 3 else None)
+                    res = f_ref[p + 1, pl.ds(r, CHUNK), :] - d_ref[p, pl.ds(r, CHUNK), :] * x + nb
                     total = res if total is None else total + res
                 rs[m, pl.ds(r, CHUNK), :] = total
             chunks(body)
         for m in range(2):
             rm[cycle, 2 + m] = 0.125 * sum_fine(rs[m])
-        for t in quarters:
-            t.wait()
-        rm[cycle, 2] += quarter[cycle, 0]
-        rm[cycle, 3] += quarter[cycle, 1]
-        rm_up = Transfer(rm.at[cycle, pl.ds(2, 2)], rm.at[cycle, pl.ds(0, 2)], 1).start()
-        rm_down = Transfer(rm.at[cycle, pl.ds(2, 2)], rm.at[cycle, pl.ds(4, 2)], -1).start()
+        swaps.append(Transfer(rm.at[cycle, pl.ds(2, 2)], rm.at[cycle, pl.ds(0, 2)], 1).start())
+        swaps.append(Transfer(rm.at[cycle, pl.ds(2, 2)], rm.at[cycle, pl.ds(4, 2)], -1).start())
         if cycle == 0:
             cm_up.wait()
             cm_down.wait()
-        rm_up.wait()
-        rm_down.wait()
+        for s in swaps:
+            s.wait()
+        rm[cycle, 0] += quarter[cycle, 1, 0]
+        rm[cycle, 1] += qown[cycle, 1]
+        rm[cycle, 2] += quarter[cycle, 0, 0]
+        rm[cycle, 3] += quarter[cycle, 0, 1]
+        rm[cycle, 4] += qown[cycle, 0]
+        rm[cycle, 5] += quarter[cycle, 1, 1]
         for q in range(6):
             ea[q + 1] = cm[q] * rm[cycle, q]
 
@@ -305,6 +323,7 @@
             total += rm[cycle, m + 2] - DAMPING / cm[m + 2] * x + 0.25 * nb
         gr[cycle, me] = 0.125 * sum_mid(total)
         gather_start(cycle, gr.at[cycle])
+        wide += share(v)
         if cycle == 0:
             gather_wait(CYCLES, gc)
         gather_wait(cycle, gr.at[cycle])
@@ -336,45 +355,44 @@
             mid_relax(eb, ea, m)
         for m in range(-1, 3):
             mid_relax(ea, eb, m)
-        up.wait()
-        down.wait()
         for m in range(-1, 3):
             e = spread_fine(ea[m + 3])
-            if m == -1:
-                @pl.when(me > 0)
-                def _():
-                    halo[kept, 0] += e
-            elif m == 2:
-                @pl.when(me < n - 1)
-                def _():
-                    halo[kept, 1] += e
-            else:
-                for p in (2 * m, 2 * m + 1):
-                    spare[p, rows, :] += e
-        for p_pair in ((0, 3), (1, 2)):
-            relax(field, spare, kept, p_pair)
-            if p_pair == (0, 3):
-                post = exchange(field)
-                post[1].start()
-                post[2].start()
-        relax_exchanged(spare, field, *post)
-        return spare, field
-
-    done, spare = vcycle(0, first, vb, va)
-    again = exchange(done)
-    again[1].start()
-    again[2].start()
-    relax_exchanged(spare, done, *again)
-    begun = exchange(spare)
-    begun[1].start()
-    begun[2].start()
-    done, spare = vcycle(1, begun, done, spare)
-    k = state["slot"]
-    last = Transfer(done.at[0, rows, :], halo.at[k, 1], -1).start()
-    for p in range(4):
-        out_ref[p] = done[p, rows, :]
-    last.wait()
-    ahead_ref[0] = halo[k, 1]
+            for p in (2 * m, 2 * m + 1):
+                v[p + 2, rows, :] += e
+
+    for t in first:
+        t.wait()
+    prepare((-1, 4))
+    relax(vb, va, (0, 3))
+    relax(vb, va, (1, 2))
+    vcycle(0, vb)
+    relax(va, vb, (-1, 0, 1))
+    relax(va, vb, (2, 3, 4))
+    relax(vd, va, (0, 1))
+    relax(vd, va, (2, 3))
+    shared = share(vd)
+    relax(va, vd, (1, 2))
+    for t in shared:
+        t.wait()
+    relax(va, vd, (0, 3))
+    relax(va, vd, (-1, 4))
+    relax(ve, va, (0, 3))
+    relax(ve, va, (1, 2))
+    vcycle(1, ve)
+    relax(va, ve, (0, 1))
+    beyond = Transfer(va.at[pl.ds(3, 1), rows, :], last, -1).start()
+    relax(va, ve, (-1, 2))
+    relax(va, ve, (3, 4))
+    relax(out_ref, va, (0, 1), raw=True)
+    relax(out_ref, va, (2, 3), raw=True)
+    beyond.wait()
+
+    def body(r):
+        at = pl.ds(r, CHUNK)
+        x, nb = neighbours(va, 4, r, None, last)
+        ahead_ref[0, at, :] = KEEP * x + c_ref[5, at, :] * (f_ref[5, at, :] + nb)
+
+    chunks(body)
 
 
 def shards(n, cotangent, counts):
@@ -383,19 +401,23 @@
     my, mz = ny // 2, nz // 2
     cy, cz = my // 4, mz
     vmem = pl.BlockSpec(memory_space=pltpu.VMEM)
-    slots = 8
+    anywhere = pl.BlockSpec(memory_space=pl.ANY)
     multiplier, following = pl.pallas_call(
         functools.partial(kernel, n),
         out_shape=(jax.ShapeDtypeStruct((nx, ny, nz), f32), jax.ShapeDtypeStruct((1, ny, nz), f32)),
-        in_specs=[vmem, vmem],
+        in_specs=[anywhere, anywhere],
         out_specs=(vmem, vmem),
         scratch_shapes=[
-            pltpu.VMEM((nx, ny + 2 * PAD, nz), f32),
-            pltpu.VMEM((nx, ny + 2 * PAD, nz), f32),
+            pltpu.VMEM((nx + 2, ny, nz), f32),
+            pltpu.VMEM((nx + 2, ny, nz), jnp.int32),
+            pltpu.VMEM((nx + 4, ny + 2 * PAD, nz), f32),
+            pltpu.VMEM((nx + 4, ny + 2 * PAD, nz), f32),
+            pltpu.VMEM((nx + 4, ny + 2 * PAD, nz), f32),
+            pltpu.VMEM((nx + 4, ny + 2 * PAD, nz), f32),
+            pltpu.VMEM((nx + 2, ny, nz), f32),
             pltpu.VMEM((nx, ny, nz), f32),
-            pltpu.VMEM((nx, ny, nz), f32),
-            pltpu.VMEM((slots, 2, ny, nz), f32),
-            pltpu.VMEM((CYCLES, 2, my, mz), f32),
+            pltpu.VMEM((1, ny, nz), f32),
+            pltpu.VMEM((CYCLES, 2, 2, my, mz), f32),
             pltpu.VMEM((2, ny, nz), f32),
             pltpu.VMEM((6, my, mz), f32),
             pltpu.VMEM((CYCLES, 6, my, mz), f32),
@@ -407,6 +429,7 @@
             pltpu.VMEM((CYCLES + 1, n, cy, cz), f32),
             pltpu.VMEM((n + 4, cy, cz), f32),
             pltpu.VMEM((n + 4, cy, cz), f32),
+            pltpu.SemaphoreType.DMA((2,)),
             pltpu.SemaphoreType.DMA((40,)),
             pltpu.SemaphoreType.DMA((40,)),
             pltpu.SemaphoreType.DMA((CYCLES + 1, n)),

time: 86.8 us -> 72.8 us (0.84)
  Pallas kernels: 81.4 us -> 67 us
    pallas_call x1, Pallas kernels: 81.4 us -> 67 us  [shards(): pl.pallas_call(functools.partial(kernel, n), out_shape=(jax.ShapeDtypeStr...]
where the time goes in v2:
time: 72.8 us; the launch traced here: 72.2 us
  Pallas kernels  67 us (92%)
  local copies, waits for them, and re-layouts  3.13 us (4%)
  other arithmetic  1.39 us (2%)
    pallas_call x1, Pallas kernels, shards(): pl.pallas_call(functools.partial(kernel, n), out_shape=(jax.ShapeDtypeStr...  67 us
    unnamed x5, local copies, waits for them, and re-layouts  2.87 us

profile of v2, /device:TPU:1, one launch (start us, length us, event | category | flops | bytes accessed | tf_op | source)
XLA Modules:
  0.0 72.2 jit_solution(17480830875430454589)
XLA Ops:
  0.6 0.0 copy-start
  0.6 1.0 %copy-done = f32[4,128,256]{2,1,0:T(8,128)S(1)} copy-done((f32[4,128,256]{2,1,0:T(8,128)S(1)}, f32[4,128,256]{2,1,0:T(8,128)}, u32[]{:S(2)}) %copy-start) | copy-done | bytes 524312
  1.7 0.0 copy-start.1
  1.7 1.0 %copy-done.1 = s32[4,128,256]{2,1,0:T(8,128)S(1)} copy-done((s32[4,128,256]{2,1,0:T(8,128)S(1)}, s32[4,128,256]{2,1,0:T(8,128)}, u32[]{:S(2)}) %copy-start.1) | copy-done | bytes 524312
  2.7 67.0 %shard_map.41 = (f32[4,128,256]{2,1,0:T(8,128)S(1)}, f32[1,128,256]{2,1,0:T(8,128)S(1)}) custom-call(f32[4,128,256]{2,1,0:T(8,128)S(1)} %copy-done, s32[4,128,256]{2,1,0:T(8,128)S(1)} %copy-done.1), custom_call_target="tpu_custom_call" | custom-call | tf_op jit(solution)/shard_map/pallas_call | solution.py:405
  69.7 0.2 slice.11
  70.0 0.1 fusion
  70.1 1.2 %pad_maximum_fusion = f32[3,4,128,256]{3,2,1,0:T(8,128)} fusion(f32[1,4,128,256]{3,2,1,0:T(8,128)S(1)} %get-tuple-element.7, f32[1,4,128,256]{3,2,1,0:T(8,128)S(1)} %get-tuple-element.8, f32[1,4,128,256]{3,2,1,0:T(8,128)S(1)} %get-tuple-element.6), kind=kLoop, calls=%fused_computation | loop fusion | flops 786432 | bytes 3145728 | tf_op jit(solution)/shard_map/stack | solution.py:444
  71.4 0.8 %copy.5 = f32[4,128,256]{2,1,0:T(8,128)} copy(f32[4,128,256]{2,1,0:T(8,128)S(1)} %get-tuple-element.11) | data formatting | bytes 1048576
  (2 shorter events, 0.1 us)
Async XLA Ops:
  0.6 1.0 %copy-start = (f32[4,128,256]{2,1,0:T(8,128)S(1)}, f32[4,128,256]{2,1,0:T(8,128)}, u32[]{:S(2)}) copy-start(f32[4,128,256]{2,1,0:T(8,128)} %f_hbm.1) | copy-start | bytes 1572868
  1.7 1.0 %copy-start.1 = (s32[4,128,256]{2,1,0:T(8,128)S(1)}, s32[4,128,256]{2,1,0:T(8,128)}, u32[]{:S(2)}) copy-start(s32[4,128,256]{2,1,0:T(8,128)} %counts_hbm.1) | copy-start | bytes 1572868

commit v3 on v2

--- a/solution.py
+++ b/solution.py
@@ -15,7 +15,7 @@
 RATE = 0.004
 MESH = pl.DeviceIdType.MESH
 PAD = 8
-CHUNK = 32
+CHUNK = 128
 
 
 def dot(a, b):
@@ -314,8 +314,6 @@
 
         for m in range(-1, 3):
             mid_relax(e2.at[cycle], ea, m)
-        wide = [Transfer(e2.at[cycle, a], e2.at[cycle, b], dist).start()
-                for a, b, dist in ((3, 1, 1), (4, 6, -1), (4, 0, 2), (3, 7, -2))]
         total = 0.0
         for m in range(2):
             x = e2[cycle, m + 3]
@@ -323,7 +321,9 @@
             total += rm[cycle, m + 2] - DAMPING / cm[m + 2] * x + 0.25 * nb
         gr[cycle, me] = 0.125 * sum_mid(total)
         gather_start(cycle, gr.at[cycle])
-        wide += share(v)
+        wide = [Transfer(e2.at[cycle, a], e2.at[cycle, b], dist).start()
+                for a, b, dist in ((3, 1, 1), (4, 6, -1), (4, 0, 2), (3, 7, -2))]
+        both = share(v)
         if cycle == 0:
             gather_wait(CYCLES, gc)
         gather_wait(cycle, gr.at[cycle])
@@ -344,7 +344,7 @@
         lax.fori_loop(0, (COARSE - 1) // 2, twice, 0)
         coarse_sweep(xb, xa)
 
-        for t in wide:
+        for t in wide + both:
             t.wait()
         for j in range(5):
             e = spread_mid(xb[me + j])
@@ -360,11 +360,11 @@
             for p in (2 * m, 2 * m + 1):
                 v[p + 2, rows, :] += e
 
+    relax(vb, va, (1, 2))
     for t in first:
         t.wait()
     prepare((-1, 4))
     relax(vb, va, (0, 3))
-    relax(vb, va, (1, 2))
     vcycle(0, vb)
     relax(va, vb, (-1, 0, 1))
     relax(va, vb, (2, 3, 4))

time: 72.8 us -> 69.3 us (0.952)
  Pallas kernels: 67 us -> 63.9 us
    pallas_call x1, Pallas kernels: 67 us -> 63.9 us  [shards(): pl.pallas_call(functools.partial(kernel, n), out_shape=(jax.ShapeDtypeStr...]
where the time goes in v3:
time: 69.3 us; the launch traced here: 69.1 us
  Pallas kernels  63.9 us (92%)
  local copies, waits for them, and re-layouts  3.13 us (5%)
  other arithmetic  1.39 us (2%)
    pallas_call x1, Pallas kernels, shards(): pl.pallas_call(functools.partial(kernel, n), out_shape=(jax.ShapeDtypeStr...  63.9 us
    unnamed x5, local copies, waits for them, and re-layouts  2.87 us
    another operation x2, other arithmetic, shards(): jnp.stack([multiplier - ahead_x, multiplier - ahead_y, multiplier - ahead...  1.39 us

profile of v3, /device:TPU:1, one launch (start us, length us, event | category | flops | bytes accessed | tf_op | source)
XLA Modules:
  0.0 69.1 jit_solution(5446112842676959291)
XLA Ops:
  0.6 0.0 copy-start
  0.6 1.0 %copy-done = f32[4,128,256]{2,1,0:T(8,128)S(1)} copy-done((f32[4,128,256]{2,1,0:T(8,128)S(1)}, f32[4,128,256]{2,1,0:T(8,128)}, u32[]{:S(2)}) %copy-start) | copy-done | bytes 524312
  1.7 0.0 copy-start.1
  1.7 1.0 %copy-done.1 = s32[4,128,256]{2,1,0:T(8,128)S(1)} copy-done((s32[4,128,256]{2,1,0:T(8,128)S(1)}, s32[4,128,256]{2,1,0:T(8,128)}, u32[]{:S(2)}) %copy-start.1) | copy-done | bytes 524312
  2.7 63.9 %shard_map.41 = (f32[4,128,256]{2,1,0:T(8,128)S(1)}, f32[1,128,256]{2,1,0:T(8,128)S(1)}) custom-call(f32[4,128,256]{2,1,0:T(8,128)S(1)} %copy-done, s32[4,128,256]{2,1,0:T(8,128)S(1)} %copy-done.1), custom_call_target="tpu_custom_call" | custom-call | tf_op jit(solution)/shard_map/pallas_call | solution.py:405
  66.7 0.2 slice.11
  66.9 0.1 fusion
  67.0 1.2 %pad_maximum_fusion = f32[3,4,128,256]{3,2,1,0:T(8,128)} fusion(f32[1,4,128,256]{3,2,1,0:T(8,128)S(1)} %get-tuple-element.7, f32[1,4,128,256]{3,2,1,0:T(8,128)S(1)} %get-tuple-element.8, f32[1,4,128,256]{3,2,1,0:T(8,128)S(1)} %get-tuple-element.6), kind=kLoop, calls=%fused_computation | loop fusion | flops 786432 | bytes 3145728 | tf_op jit(solution)/shard_map/stack | solution.py:444
  68.3 0.8 %copy.5 = f32[4,128,256]{2,1,0:T(8,128)} copy(f32[4,128,256]{2,1,0:T(8,128)S(1)} %get-tuple-element.11) | data formatting | bytes 1048576
  (2 shorter events, 0.1 us)
Async XLA Ops:
  0.6 1.0 %copy-start = (f32[4,128,256]{2,1,0:T(8,128)S(1)}, f32[4,128,256]{2,1,0:T(8,128)}, u32[]{:S(2)}) copy-start(f32[4,128,256]{2,1,0:T(8,128)} %f_hbm.1) | copy-start | bytes 1572868
  1.7 1.0 %copy-start.1 = (s32[4,128,256]{2,1,0:T(8,128)S(1)}, s32[4,128,256]{2,1,0:T(8,128)}, u32[]{:S(2)}) copy-start(s32[4,128,256]{2,1,0:T(8,128)} %counts_hbm.1) | copy-start | bytes 1572868
